TPU v7x, 128 devices: a whole 4x4x4 slice. The times are simulated.
128 devices in a mesh: wide: 8 (over y, core), col: 16 (over z, x).
Axes of the slice: x: 4, y: 4, z: 4, core: 2. Of those that a mesh axis runs over, the one named last changes fastest.
Arguments:
- rhs: float32 [98304, 256], P(('wide', 'col')), may hold values from -6 to 6
- basis: bfloat16 [98304, 256], P(('wide', 'col')), may hold values from -0.21875 to 0.21875
- self_block: bfloat16 [98304, 768], P(('wide', 'col'))
- near_block: bfloat16 [128, 8, 768, 768], P(('wide', 'col')), may hold values from -0.0546875 to 0.0546875
- near_ids: int32 [128, 8], P(('wide', 'col')), may hold values from -1 to 127, as said below
- couplings: bfloat16 [128, 40, 256, 256], P(('wide', 'col')), may hold values from -0.09375 to 0.09375
- far_ids: int32 [128, 40], P(('wide', 'col')), may hold values from -1 to 127, as said below
- intersection_start: int32 [128, 2], P(('wide', 'col')), may hold values from 0 to 512
- schwarz_inverse: bfloat16 [128, 1280, 1280], P(('wide', 'col'))
Outputs:
- solution: float32 [98304, 256], P(('wide', 'col'))
Inputs may be any that keep to these rules, and one draw needn't show every extreme that they name: `near_ids`: row c lists every cluster adjacent to cluster c on the grid (larger index distance 1; id = first index * 16 + second), ids first and -1 after them; rows of corner and edge clusters end in -1. `far_ids`: row c lists distinct clusters whose larger grid index distance from cluster c is 2 to 3, ids first and -1 after them; counts are ragged, and some rows list every such cluster. `intersection_start`: column 0 starts the rows taken by the domain of the cluster before along the second grid index, column 1 those taken by the one after.
All inputs are finite; a program needn't handle non-finite values.
Results may differ from a plain program's by a relative error of at most 0.0025.
The roundings to bfloat16 on the way count: a program that leaves them out, or rounds other values in their place, can miss the bound.
Values may be sent and summed in bfloat16 or wider, within the bound.
A program may use at most 128 MiB of HBM per device.

v0:
```python
import jax
import jax.numpy as jnp
from jax import lax
from jax.sharding import PartitionSpec as P

REACH = 3
ITERS = 2
HIGHEST_PREC = lax.Precision.HIGHEST
GROUP_SLOTS = 8


def passed_along(block, axis, distance):
    devices = range(lax.axis_size(axis))
    route = [(i - distance, i) for i in devices if i - distance in devices]
    return lax.ppermute(block, axis, route)


def with_halo(block, sides, width):
    for axis, dim in sides:
        count = lax.axis_size(axis)
        forward = [(i, i + 1) for i in range(count - 1)]
        backward = [(target, source) for source, target in forward]
        low = lax.ppermute(
            lax.slice_in_dim(block, block.shape[dim] - width, None, axis=dim), axis, forward
        )
        high = lax.ppermute(lax.slice_in_dim(block, 0, width, axis=dim), axis, backward)
        block = jnp.concatenate([low, block, high], axis=dim)
    return block


def local_gram(left, right):
    return lax.dot_general(
        left,
        right,
        (((0,), (0,)), ((), ())),
        precision=HIGHEST_PREC,
        preferred_element_type=jnp.float32,
    )


def lower_solve(factor, matrix):
    return lax.linalg.triangular_solve(
        factor, matrix, left_side=False, lower=True, transpose_a=True
    )


def far_window(coefficients):
    strip_row = jnp.stack(
        [
            coefficients if offset == 0 else passed_along(coefficients, "col", -offset)
            for offset in range(-REACH, REACH + 1)
        ]
    )
    window = jnp.stack(
        [
            strip_row if offset == 0 else passed_along(strip_row, "wide", -offset)
            for offset in range(-REACH, REACH + 1)
        ]
    )
    return window


def operate(vector_in, basis, self_block, near_block, near_ids, couplings, far_ids):
    rounded = vector_in.astype(jnp.bfloat16)
    cluster_rows, width = rounded.shape
    rank = basis.shape[1]
    wide_pos = lax.axis_index("wide")
    col_pos = lax.axis_index("col")
    col_count = lax.axis_size("col")
    result = jnp.dot(self_block, rounded, preferred_element_type=jnp.float32)
    beside_all = with_halo(rounded[None, None], (("wide", 0), ("col", 1)), 1)
    for slot_index in range(near_ids.shape[1]):
        neighbour = near_ids[0, slot_index]
        safe_id = jnp.maximum(neighbour, 0)
        wide_off = safe_id // col_count - wide_pos + 1
        col_off = safe_id % col_count - col_pos + 1
        other = lax.dynamic_slice(
            beside_all, (wide_off, col_off, 0, 0), (1, 1, cluster_rows, width)
        )[0, 0]
        product = jnp.dot(near_block[0, slot_index], other, preferred_element_type=jnp.float32)
        result = result + jnp.where(neighbour >= 0, product, jnp.zeros_like(product))
    coefficients = lax.dot_general(
        basis, rounded, (((0,), (0,)), ((), ())), preferred_element_type=jnp.float32
    ).astype(jnp.bfloat16)
    window = far_window(coefficients)
    span = 2 * REACH + 1
    flat_window = window.reshape(span * span, rank, width)
    far_list = far_ids[0]
    live_count = jnp.sum((far_list >= 0).astype(jnp.int32))
    group_count = (live_count + GROUP_SLOTS - 1) // GROUP_SLOTS

    def add_group(group_index, running):
        first_slot = group_index * GROUP_SLOTS
        targets = lax.dynamic_slice_in_dim(far_list, first_slot, GROUP_SLOTS, 0)
        safe_ids = jnp.maximum(targets, 0)
        flat_index = (safe_ids // col_count - wide_pos + REACH) * span + (
            safe_ids % col_count - col_pos + REACH
        )
        pieces_in = jnp.take(flat_window, flat_index, axis=0)
        coupling_group = lax.dynamic_slice_in_dim(couplings[0], first_slot, GROUP_SLOTS, 0)
        live_slots = (targets >= 0)[:, None, None]
        coupling_group = jnp.where(live_slots, coupling_group, jnp.zeros_like(coupling_group))
        return running + jnp.einsum(
            "lrs,lsk->rk", coupling_group, pieces_in, preferred_element_type=jnp.float32
        )

    far_sum = lax.fori_loop(0, group_count, add_group, jnp.zeros((rank, width), jnp.float32))
    return result + jnp.dot(basis, far_sum.astype(jnp.bfloat16), preferred_element_type=jnp.float32)


def add_rows(matrix, addend, start):
    current = lax.dynamic_slice_in_dim(matrix, start, addend.shape[0], 0)
    return lax.dynamic_update_slice_in_dim(matrix, current + addend, start, 0)


def precondition(vector_in, intersection_start, schwarz_inverse):
    rounded = vector_in.astype(jnp.bfloat16)
    cluster_rows = rounded.shape[0]
    margin = (schwarz_inverse.shape[1] - cluster_rows) // 2
    starts = intersection_start[0]
    prev_whole, prev_starts = passed_along((rounded, intersection_start), "col", 1)
    next_whole, next_starts = passed_along((rounded, intersection_start), "col", -1)
    prev_rows = lax.dynamic_slice_in_dim(prev_whole, prev_starts[0, 1], margin, 0)
    next_rows = lax.dynamic_slice_in_dim(next_whole, next_starts[0, 0], margin, 0)
    domain = jnp.concatenate([prev_rows, rounded, next_rows], axis=0)
    solved = jnp.dot(schwarz_inverse[0], domain, preferred_element_type=jnp.float32)
    result = solved[margin : margin + cluster_rows]
    from_next = passed_along(solved[:margin], "col", -1)
    from_prev = passed_along(solved[margin + cluster_rows :], "col", 1)
    result = add_rows(result, from_next, starts[1])
    result = add_rows(result, from_prev, starts[0])
    return result


def on_device(
    rhs,
    basis,
    self_block,
    near_block,
    near_ids,
    couplings,
    far_ids,
    intersection_start,
    schwarz_inverse,
):
    width = rhs.shape[1]
    first_sum = lax.psum(local_gram(rhs, rhs), ("wide", "col"))
    factor = jnp.linalg.cholesky(first_sum)
    beta_block = factor.T
    bases = [lower_solve(factor, rhs)]
    directions = []
    columns = []
    for iteration in range(ITERS):
        precond_out = precondition(bases[-1], intersection_start, schwarz_inverse)
        image = operate(precond_out, basis, self_block, near_block, near_ids, couplings, far_ids)
        stacked = jnp.concatenate(bases, axis=1)
        projected = lax.psum(local_gram(stacked, image), ("wide", "col"))
        image = image - jnp.dot(stacked, projected, precision=HIGHEST_PREC)
        gram_sum = lax.psum(local_gram(image, image), ("wide", "col"))
        factor = jnp.linalg.cholesky(gram_sum)
        columns.append((projected, factor.T))
        directions.append(precond_out)
        if iteration + 1 < ITERS:
            bases.append(lower_solve(factor, image))
    hessen = jnp.zeros(((ITERS + 1) * width, ITERS * width), jnp.float32)
    for column_index, (projected, sub_block) in enumerate(columns):
        upper_rows = (column_index + 1) * width
        hessen = hessen.at[:upper_rows, column_index * width : (column_index + 1) * width].set(
            projected
        )
        hessen = hessen.at[
            upper_rows : upper_rows + width, column_index * width : (column_index + 1) * width
        ].set(sub_block)
    normal_matrix = jnp.dot(hessen.T, hessen, precision=HIGHEST_PREC)
    target = jnp.dot(hessen[:width].T, beta_block, precision=HIGHEST_PREC)
    small_factor = jnp.linalg.cholesky(normal_matrix)
    middle = lax.linalg.triangular_solve(small_factor, target, left_side=True, lower=True)
    weights_y = lax.linalg.triangular_solve(
        small_factor, middle, left_side=True, lower=True, transpose_a=True
    )
    return jnp.dot(jnp.concatenate(directions, axis=1), weights_y, precision=HIGHEST_PREC)


def solution(mesh):
    in_specs = (
        P(("wide", "col"), None),
        P(("wide", "col"), None),
        P(("wide", "col"), None),
        P(("wide", "col"), None, None, None),
        P(("wide", "col"), None),
        P(("wide", "col"), None, None, None),
        P(("wide", "col"), None),
        P(("wide", "col"), None),
        P(("wide", "col"), None, None),
    )
    out_specs = P(("wide", "col"), None)
    return jax.shard_map(
        on_device, mesh=mesh, in_specs=in_specs, out_specs=out_specs, check_vma=False
    )
```

profile of v0, /device:TPU:1, one launch (start us, length us, event | category | flops | bytes accessed | tf_op | source)
XLA Modules:
  0.0 1556.4 jit_solution(12817224653365156530)
XLA Ops:
  10.3 146.7 %all-reduce.9.cloned.1.call-done = f32[256,256]{0,1:T(8,128)} async-done(((f32[256,256]{0,1:T(8,128)}), f32[256,256]{0,1:T(8,128)}) %all-reduce.9.cloned.1.call-update) | async-done | bytes 262160 | tf_op jit(solution)/shard_map/psum | solution.py:147
  159.7 11.7 cholesky.392
  172.1 10.4 custom-call.47
  186.2 13.2 cholesky.402
  203.7 7.4 while.36
  211.1 21.1 %custom-call.48 = f32[2,128,128]{1,2,0:T(8,128)} custom-call(f32[2,128,128]{2,1,0:T(8,128)} %get-tuple-element.295), custom_call_target="InvertDiagBlocksLowerTriangular" | custom-call | tf_op jit(solution)/shard_map/triangular_solve/custom-call.9 | solution.py:42
  242.7 4.0 collective-permute-start.1
  260.9 4.7 collective-permute-start.5
  281.5 8.3 collective-permute-start.10
  309.5 7.1 collective-permute-start.16
  339.1 19.0 %collective-permute-done.6 = bf16[1,1,768,256]{2,3,1,0:T(8,128)(2,1)} collective-permute-done((bf16[1,1,768,256]{2,3,1,0:T(8,128)(2,1)}, bf16[1,1,768,256]{2,3,1,0:T(8,128)(2,1)}, u32[]{:S(2)}, u32[]{:S(2)}) %collective-permute-start.6) | collective-permute-done | bytes 393248 | tf_op jit(solution)/shard_map/ppermute | solution.py:23
  367.2 5.0 collective-permute-start.8
  387.8 9.3 copy.13
  397.9 14.7 while.33
  398.0 4.4 gather_fusion
  405.4 4.4 gather_fusion
  428.6 185.3 %all-reduce.11.cloned.1.call-done = f32[256,256]{1,0:T(8,128)} async-done(((f32[256,256]{1,0:T(8,128)}), f32[256,256]{1,0:T(8,128)}) %all-reduce.11.cloned.1.call-update) | async-done | bytes 262160 | tf_op jit(solution)/shard_map/psum | solution.py:157
  618.9 138.9 %all-reduce.13.cloned.1.call-done = f32[256,256]{0,1:T(8,128)} async-done(((f32[256,256]{0,1:T(8,128)}), f32[256,256]{0,1:T(8,128)}) %all-reduce.13.cloned.1.call-update) | async-done | bytes 262160 | tf_op jit(solution)/shard_map/psum | solution.py:159
  762.0 13.2 cholesky.419
  778.2 11.3 custom-call.49
  792.9 13.2 cholesky.429
  812.6 7.5 while.37
  820.2 21.1 %custom-call.50 = f32[2,128,128]{1,2,0:T(8,128)} custom-call(f32[2,128,128]{2,1,0:T(8,128)} %get-tuple-element.296), custom_call_target="InvertDiagBlocksLowerTriangular" | custom-call | tf_op jit(solution)/shard_map/triangular_solve/custom-call.9 | solution.py:42
  850.6 6.0 collective-permute-done.22
  863.1 4.4 collective-permute-start.25
  875.1 9.7 collective-permute-start.30
  896.6 4.8 collective-permute-done.34
  904.8 8.3 collective-permute-start.36
  922.9 30.5 %collective-permute-done.26 = bf16[1,1,768,256]{2,3,1,0:T(8,128)(2,1)S(1)} collective-permute-done((bf16[1,1,768,256]{2,3,1,0:T(8,128)(2,1)S(1)}, bf16[1,1,768,256]{2,3,1,0:T(8,128)(2,1)S(1)}, u32[]{:S(2)}, u32[]{:S(2)}) %collective-permute-start.26) | collective-permute-done | bytes 393248 | tf_op jit(solution)/shard_map/ppermute | solution.py:23
  961.2 5.0 collective-permute-start.28
  983.0 9.3 copy.19
  993.1 12.1 while.34
  1023.1 184.5 %all-reduce.15.cloned.1.call-done = f32[512,256]{1,0:T(8,128)} async-done(((f32[512,256]{1,0:T(8,128)}), f32[512,256]{1,0:T(8,128)}) %all-reduce.15.cloned.1.call-update) | async-done | bytes 524304 | tf_op jit(solution)/shard_map/psum | solution.py:157
  1215.5 6.3 scatter.16
  1221.8 131.3 %all-reduce.17.cloned.1.call-done = f32[256,256]{0,1:T(8,128)} async-done(((f32[256,256]{0,1:T(8,128)}), f32[256,256]{0,1:T(8,128)}) %all-reduce.17.cloned.1.call-update) | async-done | bytes 262160 | tf_op jit(solution)/shard_map/psum | solution.py:159
  1355.2 11.7 cholesky.446
  1367.0 9.8 custom-call.51
  1377.2 11.7 cholesky.456
  1397.7 11.7 cholesky.167
  1409.5 9.8 custom-call.37
  1421.9 11.9 cholesky.190
  1435.1 9.8 custom-call.38
  1446.5 11.7 cholesky.294
  1459.0 9.8 custom-call.52
  1470.2 11.9 cholesky.307
  1485.6 10.6 while.35
  1496.2 40.2 %custom-call.39 = f32[4,128,128]{1,2,0:T(8,128)S(1)} custom-call(f32[4,128,128]{2,1,0:T(8,128)} %get-tuple-element.288), custom_call_target="InvertDiagBlocksLowerTriangular" | custom-call | tf_op jit(solution)/shard_map/triangular_solve | solution.py:178
  1544.8 4.9 fusion.36
  (391 shorter events, 310.4 us)
Async XLA Ops:
  6.5 150.4 %all-reduce.9.cloned.1.call-start = ((), (), s32[]{:S(2)}) async-start(), calls=%async_computation | async-start | bytes 524288 | tf_op jit(solution)/shard_map/psum | solution.py:147
  10.2 603.7 %all-reduce.11.cloned.1.call-start = ((), (), s32[]{:S(2)}) async-start(), calls=%async_computation.1 | async-start | bytes 524288 | tf_op jit(solution)/shard_map/psum | solution.py:157
  238.0 15.6 %collective-permute-start = (bf16[768,256]{0,1:T(8,128)(2,1)}, bf16[768,256]{0,1:T(8,128)(2,1)}, u32[]{:S(2)}, u32[]{:S(2)}) collective-permute-start(bf16[768,256]{0,1:T(8,128)(2,1)} %fusion.109), channel_id=1, source_target_pairs={{0,1},{1,2},{2,3},{3,4},{4,5},{5,6},{6,7},{7,8},{8,9},{9,10},{10,1... | collective-permute-start | bytes 1179656 | tf_op jit(solution)/shard_map/ppermute | solution.py:15
  241.4 13.3 collective-permute-start.2
  242.7 5.6 collective-permute-start.1
  246.7 6.2 collective-permute-start.3
  259.6 11.3 collective-permute-start.4
  260.9 14.9 collective-permute-start.5
  281.5 15.3 collective-permute-start.10
  289.8 9.0 collective-permute-start.11
  291.1 8.4 collective-permute-start.12
  294.2 6.9 collective-permute-start.13
  295.5 9.3 collective-permute-start.14
  296.8 12.0 collective-permute-start.15
  309.5 54.3 %collective-permute-start.16 = (bf16[7,256,256]{1,2,0:T(8,128)(2,1)}, bf16[7,256,256]{1,2,0:T(8,128)(2,1)}, u32[]{:S(2)}, u32[]{:S(2)}) collective-permute-start(bf16[7,256,256]{1,2,0:T(8,128)(2,1)} %bitcast_dynamic-update-slice_fusion.25), channel_id=1, source_target_pairs={{0,48},{16,64},{32,80},{48,96},{64,112},{1,49},{17,65},{33,81},{49... | collective-permute-start | bytes 2752520 | tf_op jit(solution)/shard_map/ppermute | solution.py:15
  316.5 50.7 %collective-permute-start.17 = (bf16[7,256,256]{1,2,0:T(8,128)(2,1)}, bf16[7,256,256]{1,2,0:T(8,128)(2,1)}, u32[]{:S(2)}, u32[]{:S(2)}) collective-permute-start(bf16[7,256,256]{1,2,0:T(8,128)(2,1)} %bitcast_dynamic-update-slice_fusion.25), channel_id=1, source_target_pairs={{0,32},{16,48},{32,64},{48,80},{64,96},{80,112},{1,33},{17,49},{33... | collective-permute-start | bytes 2752520 | tf_op jit(solution)/shard_map/ppermute | solution.py:15
  319.5 38.6 %collective-permute-start.6 = (bf16[1,1,768,256]{2,3,1,0:T(8,128)(2,1)}, bf16[1,1,768,256]{2,3,1,0:T(8,128)(2,1)}, u32[]{:S(2)}, u32[]{:S(2)}) collective-permute-start(bf16[1,1,768,256]{2,3,1,0:T(8,128)(2,1)} %convert_bitcast_fusion.1), channel_id=1, source_target_pairs={{0,16},{16,32},{32,48},{48,64},{64,80},{80,96},{96,112},{1,17},{17... | collective-permute-start | bytes 1179656 | tf_op jit(solution)/shard_map/ppermute | solution.py:23
  321.5 38.6 %collective-permute-start.7 = (bf16[1,1,768,256]{2,3,1,0:T(8,128)(2,1)}, bf16[1,1,768,256]{2,3,1,0:T(8,128)(2,1)}, u32[]{:S(2)}, u32[]{:S(2)}) collective-permute-start(bf16[1,1,768,256]{2,3,1,0:T(8,128)(2,1)} %convert_bitcast_fusion.1), channel_id=1, source_target_pairs={{16,0},{32,16},{48,32},{64,48},{80,64},{96,80},{112,96},{17,1},{33... | collective-permute-start | bytes 1179656 | tf_op jit(solution)/shard_map/ppermute | solution.py:26
  324.6 49.8 %collective-permute-start.18 = (bf16[7,256,256]{1,2,0:T(8,128)(2,1)}, bf16[7,256,256]{1,2,0:T(8,128)(2,1)}, u32[]{:S(2)}, u32[]{:S(2)}) collective-permute-start(bf16[7,256,256]{1,2,0:T(8,128)(2,1)} %bitcast_dynamic-update-slice_fusion.25), channel_id=1, source_target_pairs={{0,16},{16,32},{32,48},{48,64},{64,80},{80,96},{96,112},{1,17},{17... | collective-permute-start | bytes 2752520 | tf_op jit(solution)/shard_map/ppermute | solution.py:15
  358.2 23.7 %collective-permute-start.19 = (bf16[7,256,256]{1,2,0:T(8,128)(2,1)}, bf16[7,256,256]{1,2,0:T(8,128)(2,1)S(1)}, u32[]{:S(2)}, u32[]{:S(2)}) collective-permute-start(bf16[7,256,256]{1,2,0:T(8,128)(2,1)} %bitcast_dynamic-update-slice_fusion.25), channel_id=1, source_target_pairs={{16,0},{32,16},{48,32},{64,48},{80,64},{96,80},{112,96},{17,1},{33... | collective-permute-start | bytes 2752520 | tf_op jit(solution)/shard_map/ppermute | solution.py:15
  360.1 25.7 %collective-permute-start.20 = (bf16[7,256,256]{1,2,0:T(8,128)(2,1)}, bf16[7,256,256]{1,2,0:T(8,128)(2,1)S(1)}, u32[]{:S(2)}, u32[]{:S(2)}) collective-permute-start(bf16[7,256,256]{1,2,0:T(8,128)(2,1)} %bitcast_dynamic-update-slice_fusion.25), channel_id=1, source_target_pairs={{32,0},{48,16},{64,32},{80,48},{96,64},{112,80},{33,1},{49,17},{65... | collective-permute-start | bytes 2752520 | tf_op jit(solution)/shard_map/ppermute | solution.py:15
  363.8 23.0 %collective-permute-start.21 = (bf16[7,256,256]{1,2,0:T(8,128)(2,1)}, bf16[7,256,256]{1,2,0:T(8,128)(2,1)S(1)}, u32[]{:S(2)}, u32[]{:S(2)}) collective-permute-start(bf16[7,256,256]{1,2,0:T(8,128)(2,1)} %bitcast_dynamic-update-slice_fusion.25), channel_id=1, source_target_pairs={{48,0},{64,16},{80,32},{96,48},{112,64},{49,1},{65,17},{81,33},{97... | collective-permute-start | bytes 2752520 | tf_op jit(solution)/shard_map/ppermute | solution.py:15
  367.2 45.4 %collective-permute-start.8 = (bf16[3,1,768,256]{2,3,1,0:T(8,128)(2,1)}, bf16[3,1,768,256]{2,3,1,0:T(8,128)(2,1)}, u32[]{:S(2)}, u32[]{:S(2)}) collective-permute-start(bf16[3,1,768,256]{2,3,1,0:T(8,128)(2,1)} %pad_maximum_fusion.2), channel_id=1, source_target_pairs={{0,1},{1,2},{2,3},{3,4},{4,5},{5,6},{6,7},{7,8},{8,9},{9,10},{10,1... | collective-permute-start | bytes 3538952 | tf_op jit(solution)/shard_map/ppermute | solution.py:23
  374.4 38.2 %collective-permute-start.9 = (bf16[3,1,768,256]{2,3,1,0:T(8,128)(2,1)}, bf16[3,1,768,256]{2,3,1,0:T(8,128)(2,1)}, u32[]{:S(2)}, u32[]{:S(2)}) collective-permute-start(bf16[3,1,768,256]{2,3,1,0:T(8,128)(2,1)} %pad_maximum_fusion.2), channel_id=1, source_target_pairs={{1,0},{2,1},{3,2},{4,3},{5,4},{6,5},{7,6},{8,7},{9,8},{10,9},{11,1... | collective-permute-start | bytes 3538952 | tf_op jit(solution)/shard_map/ppermute | solution.py:26
  428.5 384.1 %copy-start.38 = (s32[2,2]{1,0:T(2,128)S(1)}, s32[2,2]{1,0:T(2,128)}, u32[]{:S(2)}) copy-start(s32[2,2]{1,0:T(2,128)} %copy-done.37) | copy-start | bytes 52
  428.5 329.3 %all-reduce.13.cloned.1.call-start = ((), (), s32[]{:S(2)}) async-start(), calls=%async_computation.2 | async-start | bytes 524288 | tf_op jit(solution)/shard_map/psum | solution.py:159
  618.6 589.0 %all-reduce.15.cloned.1.call-start = ((), (), s32[]{:S(2)}) async-start(), calls=%async_computation.3 | async-start | bytes 1048576 | tf_op jit(solution)/shard_map/psum | solution.py:157
  846.6 9.9 collective-permute-start.22
  849.3 11.2 collective-permute-start.23
  861.6 8.4 collective-permute-start.24
  863.1 9.3 collective-permute-start.25
  875.1 16.7 %collective-permute-start.30 = (bf16[256,256]{0,1:T(8,128)(2,1)S(1)}, bf16[256,256]{0,1:T(8,128)(2,1)S(1)}, u32[]{:S(2)}, u32[]{:S(2)}) collective-permute-start(bf16[256,256]{0,1:T(8,128)(2,1)S(1)} %bitcast.418), channel_id=1, source_target_pairs={{0,3},{1,4},{2,5},{3,6},{4,7},{5,8},{6,9},{7,10},{8,11},{9,12},{10... | collective-permute-start | bytes 393224 | tf_op jit(solution)/shard_map/ppermute | solution.py:15
  884.8 9.0 collective-permute-start.31
  886.4 8.1 collective-permute-start.32
  889.2 6.7 collective-permute-start.33
  890.5 10.8 collective-permute-start.34
  891.8 12.3 collective-permute-start.35
  904.8 52.9 %collective-permute-start.36 = (bf16[7,256,256]{1,2,0:T(8,128)(2,1)}, bf16[7,256,256]{1,2,0:T(8,128)(2,1)}, u32[]{:S(2)}, u32[]{:S(2)}) collective-permute-start(bf16[7,256,256]{1,2,0:T(8,128)(2,1)} %bitcast_dynamic-update-slice_fusion.19), channel_id=1, source_target_pairs={{0,48},{16,64},{32,80},{48,96},{64,112},{1,49},{17,65},{33,81},{49... | collective-permute-start | bytes 2752520 | tf_op jit(solution)/shard_map/ppermute | solution.py:15
  913.1 48.1 %collective-permute-start.37 = (bf16[7,256,256]{1,2,0:T(8,128)(2,1)}, bf16[7,256,256]{1,2,0:T(8,128)(2,1)}, u32[]{:S(2)}, u32[]{:S(2)}) collective-permute-start(bf16[7,256,256]{1,2,0:T(8,128)(2,1)} %bitcast_dynamic-update-slice_fusion.19), channel_id=1, source_target_pairs={{0,32},{16,48},{32,64},{48,80},{64,96},{80,112},{1,33},{17,49},{33... | collective-permute-start | bytes 2752520 | tf_op jit(solution)/shard_map/ppermute | solution.py:15
  915.3 38.0 %collective-permute-start.26 = (bf16[1,1,768,256]{2,3,1,0:T(8,128)(2,1)S(1)}, bf16[1,1,768,256]{2,3,1,0:T(8,128)(2,1)S(1)}, u32[]{:S(2)}, u32[]{:S(2)}) collective-permute-start(bf16[1,1,768,256]{2,3,1,0:T(8,128)(2,1)S(1)} %convert_bitcast_fusion), channel_id=1, source_target_pairs={{0,16},{16,32},{32,48},{48,64},{64,80},{80,96},{96,112},{1,17},{17... | collective-permute-start | bytes 1179656 | tf_op jit(solution)/shard_map/ppermute | solution.py:23
  917.3 38.0 %collective-permute-start.27 = (bf16[1,1,768,256]{2,3,1,0:T(8,128)(2,1)S(1)}, bf16[1,1,768,256]{2,3,1,0:T(8,128)(2,1)S(1)}, u32[]{:S(2)}, u32[]{:S(2)}) collective-permute-start(bf16[1,1,768,256]{2,3,1,0:T(8,128)(2,1)S(1)} %convert_bitcast_fusion), channel_id=1, source_target_pairs={{16,0},{32,16},{48,32},{64,48},{80,64},{96,80},{112,96},{17,1},{33... | collective-permute-start | bytes 1179656 | tf_op jit(solution)/shard_map/ppermute | solution.py:26
  919.7 48.7 %collective-permute-start.38 = (bf16[7,256,256]{1,2,0:T(8,128)(2,1)}, bf16[7,256,256]{1,2,0:T(8,128)(2,1)}, u32[]{:S(2)}, u32[]{:S(2)}) collective-permute-start(bf16[7,256,256]{1,2,0:T(8,128)(2,1)} %bitcast_dynamic-update-slice_fusion.19), channel_id=1, source_target_pairs={{0,16},{16,32},{32,48},{48,64},{64,80},{80,96},{96,112},{1,17},{17... | collective-permute-start | bytes 2752520 | tf_op jit(solution)/shard_map/ppermute | solution.py:15
  953.3 23.7 %collective-permute-start.39 = (bf16[7,256,256]{1,2,0:T(8,128)(2,1)}, bf16[7,256,256]{1,2,0:T(8,128)(2,1)S(1)}, u32[]{:S(2)}, u32[]{:S(2)}) collective-permute-start(bf16[7,256,256]{1,2,0:T(8,128)(2,1)} %bitcast_dynamic-update-slice_fusion.19), channel_id=1, source_target_pairs={{16,0},{32,16},{48,32},{64,48},{80,64},{96,80},{112,96},{17,1},{33... | collective-permute-start | bytes 2752520 | tf_op jit(solution)/shard_map/ppermute | solution.py:15
  955.3 25.7 %collective-permute-start.40 = (bf16[7,256,256]{1,2,0:T(8,128)(2,1)}, bf16[7,256,256]{1,2,0:T(8,128)(2,1)S(1)}, u32[]{:S(2)}, u32[]{:S(2)}) collective-permute-start(bf16[7,256,256]{1,2,0:T(8,128)(2,1)} %bitcast_dynamic-update-slice_fusion.19), channel_id=1, source_target_pairs={{32,0},{48,16},{64,32},{80,48},{96,64},{112,80},{33,1},{49,17},{65... | collective-permute-start | bytes 2752520 | tf_op jit(solution)/shard_map/ppermute | solution.py:15
  957.7 24.2 %collective-permute-start.41 = (bf16[7,256,256]{1,2,0:T(8,128)(2,1)}, bf16[7,256,256]{1,2,0:T(8,128)(2,1)S(1)}, u32[]{:S(2)}, u32[]{:S(2)}) collective-permute-start(bf16[7,256,256]{1,2,0:T(8,128)(2,1)} %bitcast_dynamic-update-slice_fusion.19), channel_id=1, source_target_pairs={{48,0},{64,16},{80,32},{96,48},{112,64},{49,1},{65,17},{81,33},{97... | collective-permute-start | bytes 2752520 | tf_op jit(solution)/shard_map/ppermute | solution.py:15
  961.2 44.0 %collective-permute-start.28 = (bf16[3,1,768,256]{2,3,1,0:T(8,128)(2,1)}, bf16[3,1,768,256]{2,3,1,0:T(8,128)(2,1)}, u32[]{:S(2)}, u32[]{:S(2)}) collective-permute-start(bf16[3,1,768,256]{2,3,1,0:T(8,128)(2,1)} %pad_maximum_fusion.3), channel_id=1, source_target_pairs={{0,1},{1,2},{2,3},{3,4},{4,5},{5,6},{6,7},{7,8},{8,9},{9,10},{10,1... | collective-permute-start | bytes 3538952 | tf_op jit(solution)/shard_map/ppermute | solution.py:23
  968.4 36.7 %collective-permute-start.29 = (bf16[3,1,768,256]{2,3,1,0:T(8,128)(2,1)}, bf16[3,1,768,256]{2,3,1,0:T(8,128)(2,1)}, u32[]{:S(2)}, u32[]{:S(2)}) collective-permute-start(bf16[3,1,768,256]{2,3,1,0:T(8,128)(2,1)} %pad_maximum_fusion.3), channel_id=1, source_target_pairs={{1,0},{2,1},{3,2},{4,3},{5,4},{6,5},{7,6},{8,7},{9,8},{10,9},{11,1... | collective-permute-start | bytes 3538952 | tf_op jit(solution)/shard_map/ppermute | solution.py:26
  1020.4 332.6 %all-reduce.17.cloned.1.call-start = ((), (), s32[]{:S(2)}) async-start(), calls=%async_computation.4 | async-start | bytes 524288 | tf_op jit(solution)/shard_map/psum | solution.py:159
  (44 other events, 971.7 us)
Sparse Core Ops, SparseCore 0:
  12.1 144.7 all-reduce.8
  428.6 185.2 all-reduce.10
  618.8 138.9 all-reduce.12
  1020.6 186.9 all-reduce.14
  1212.9 140.1 all-reduce.16
where the time goes:
time: 1570 us; the launch traced here: 1560 us
  waiting for transfers between devices  876 us (56%)
  other arithmetic  300 us (19%)
  local copies, waits for them, and re-layouts  133 us (8%)
  starting transfers between devices  117 us (7%)
  matrix products  91.5 us (6%)
  between operations  37.7 us (2%)
    psum x2, waiting for transfers between devices, on_device(): projected = lax.psum(local_gram(stacked, image), ('wide', 'col'))  370 us
    psum x2, waiting for transfers between devices, on_device(): gram_sum = lax.psum(local_gram(image, image), ('wide', 'col'))  270 us
    psum x1, waiting for transfers between devices, on_device(): first_sum = lax.psum(local_gram(rhs, rhs), ('wide', 'col'))  147 us
    ppermute x34, starting transfers between devices, passed_along(): return lax.ppermute(block, axis, route)  94.5 us
    another operation x15, other arithmetic, on_device(): small_factor = jnp.linalg.cholesky(normal_matrix)  79.5 us
    another operation x14, other arithmetic, on_device(): factor = jnp.linalg.cholesky(gram_sum)  76.6 us
    ppermute x4, waiting for transfers between devices, with_halo(): lax.ppermute(lax.slice_in_dim(block, block.shape[dim] - width, None, axis...  49.5 us
    another operation x4, other arithmetic, lower_solve(): lax.linalg.triangular_solve(factor, matrix, left_side=False, lower=True,...  42.9 us
  transfers between devices with their start and end apart: 47, of which 22 were waited for; matrix products, arithmetic and copies ran while one was open for 7% of the time, Pallas kernels for 0%

commit v1 on v0

--- a/solution.py
+++ b/solution.py
@@ -2,6 +2,7 @@
 import jax.numpy as jnp
 from jax import lax
 from jax.sharding import PartitionSpec as P
+from jax.lax import psum
 
 REACH = 3
 ITERS = 2
@@ -154,7 +155,8 @@
         precond_out = precondition(bases[-1], intersection_start, schwarz_inverse)
         image = operate(precond_out, basis, self_block, near_block, near_ids, couplings, far_ids)
         stacked = jnp.concatenate(bases, axis=1)
-        projected = lax.psum(local_gram(stacked, image), ("wide", "col"))
+        reach_screen = lambda raw, axis_tag, group_axis: psum(psum(raw, axis_tag), group_axis)
+        projected = reach_screen(local_gram(stacked, image), "wide", "col")
         image = image - jnp.dot(stacked, projected, precision=HIGHEST_PREC)
         gram_sum = lax.psum(local_gram(image, image), ("wide", "col"))
         factor = jnp.linalg.cholesky(gram_sum)

time: 1570 us -> 1580 us (level)
    psum x2 -> x4, waiting for transfers between devices: 370 us -> 376 us  [the longest x2 202 us: on_device(): psum(raw, axis_tag)]
  transfers between devices with their start and end apart: 47 -> 49, of which waited for: 22 -> 24; matrix products, arithmetic and copies ran while one was open for 7% -> 7% of each run, Pallas kernels for 0% -> 0%
where the time goes in v1:
time: 1580 us; the launch traced here: 1570 us
  waiting for transfers between devices  886 us (56%)
  other arithmetic  300 us (19%)
  local copies, waits for them, and re-layouts  133 us (8%)
  starting transfers between devices  117 us (7%)
  matrix products  91.5 us (6%)
  between operations  38.1 us (2%)
    psum x2, waiting for transfers between devices, on_device(): gram_sum = lax.psum(local_gram(image, image), ('wide', 'col'))  275 us
    psum x2, waiting for transfers between devices, on_device(): psum(raw, axis_tag)  202 us
    psum x2, waiting for transfers between devices, on_device(): psum(psum(raw, axis_tag), group_axis)  174 us
    psum x1, waiting for transfers between devices, on_device(): first_sum = lax.psum(local_gram(rhs, rhs), ('wide', 'col'))  147 us
    ppermute x34, starting transfers between devices, passed_along(): return lax.ppermute(block, axis, route)  94.5 us
    another operation x15, other arithmetic, on_device(): small_factor = jnp.linalg.cholesky(normal_matrix)  79.5 us
    another operation x14, other arithmetic, on_device(): factor = jnp.linalg.cholesky(gram_sum)  76.6 us
    ppermute x4, waiting for transfers between devices, with_halo(): lax.ppermute(lax.slice_in_dim(block, block.shape[dim] - width, None, axis...  49.5 us
  transfers between devices with their start and end apart: 49, of which 24 were waited for; matrix products, arithmetic and copies ran while one was open for 7% of the time, Pallas kernels for 0%

profile of v1, /device:TPU:1, one launch (start us, length us, event | category | flops | bytes accessed | tf_op | source)
XLA Modules:
  0.0 1567.3 jit_solution(7804689092650001579)
XLA Ops:
  10.3 146.7 %all-reduce.11.cloned.1.call-done = f32[256,256]{0,1:T(8,128)} async-done(((f32[256,256]{0,1:T(8,128)}), f32[256,256]{0,1:T(8,128)}) %all-reduce.11.cloned.1.call-update) | async-done | bytes 262160 | tf_op jit(solution)/shard_map/psum | solution.py:148
  159.7 11.7 cholesky.392
  172.1 10.4 custom-call.47
  186.2 13.2 cholesky.402
  203.7 7.4 while.36
  211.1 21.1 %custom-call.48 = f32[2,128,128]{1,2,0:T(8,128)} custom-call(f32[2,128,128]{2,1,0:T(8,128)} %get-tuple-element.295), custom_call_target="InvertDiagBlocksLowerTriangular" | custom-call | tf_op jit(solution)/shard_map/triangular_solve/custom-call.9 | solution.py:43
  260.9 4.7 collective-permute-start.5
  281.5 8.3 collective-permute-start.10
  309.4 7.1 collective-permute-start.16
  339.1 19.0 %collective-permute-done.6 = bf16[1,1,768,256]{2,3,1,0:T(8,128)(2,1)} collective-permute-done((bf16[1,1,768,256]{2,3,1,0:T(8,128)(2,1)}, bf16[1,1,768,256]{2,3,1,0:T(8,128)(2,1)}, u32[]{:S(2)}, u32[]{:S(2)}) %collective-permute-start.6) | collective-permute-done | bytes 393248 | tf_op jit(solution)/shard_map/ppermute | solution.py:24
  367.2 5.0 collective-permute-start.8
  387.8 9.3 copy.13
  397.9 14.7 while.33
  398.0 4.4 gather_fusion
  405.4 4.4 gather_fusion
  428.5 101.6 %all-reduce.13.cloned.1.call-done = f32[256,256]{1,0:T(8,128)} async-done(((f32[256,256]{1,0:T(8,128)}), f32[256,256]{1,0:T(8,128)}) %all-reduce.13.cloned.1.call-update) | async-done | bytes 262160 | tf_op jit(solution)/shard_map/psum | solution.py:158
  530.2 87.7 %all-reduce.15.cloned.1.call-done = f32[256,256]{1,0:T(8,128)} async-done(((f32[256,256]{1,0:T(8,128)}), f32[256,256]{1,0:T(8,128)}) %all-reduce.15.cloned.1.call-update) | async-done | bytes 262160 | tf_op jit(solution)/shard_map/psum | solution.py:158
  622.9 142.0 %all-reduce.17.cloned.1.call-done = f32[256,256]{0,1:T(8,128)} async-done(((f32[256,256]{0,1:T(8,128)}), f32[256,256]{0,1:T(8,128)}) %all-reduce.17.cloned.1.call-update) | async-done | bytes 262160 | tf_op jit(solution)/shard_map/psum | solution.py:161
  769.1 13.2 cholesky.419
  785.3 11.3 custom-call.49
  800.1 13.2 cholesky.429
  819.8 7.5 while.37
  827.3 21.1 %custom-call.50 = f32[2,128,128]{1,2,0:T(8,128)} custom-call(f32[2,128,128]{2,1,0:T(8,128)} %get-tuple-element.296), custom_call_target="InvertDiagBlocksLowerTriangular" | custom-call | tf_op jit(solution)/shard_map/triangular_solve/custom-call.9 | solution.py:43
  857.7 6.0 collective-permute-done.22
  882.3 9.7 collective-permute-start.30
  903.7 4.8 collective-permute-done.34
  911.9 8.3 collective-permute-start.36
  930.0 30.5 %collective-permute-done.26 = bf16[1,1,768,256]{2,3,1,0:T(8,128)(2,1)S(1)} collective-permute-done((bf16[1,1,768,256]{2,3,1,0:T(8,128)(2,1)S(1)}, bf16[1,1,768,256]{2,3,1,0:T(8,128)(2,1)S(1)}, u32[]{:S(2)}, u32[]{:S(2)}) %collective-permute-start.26) | collective-permute-done | bytes 393248 | tf_op jit(solution)/shard_map/ppermute | solution.py:24
  968.3 5.0 collective-permute-start.28
  990.1 9.3 copy.19
  1000.2 12.1 while.34
  1027.6 100.5 %all-reduce.19.cloned.1.call-done = f32[512,256]{1,0:T(8,128)} async-done(((f32[512,256]{1,0:T(8,128)}), f32[512,256]{1,0:T(8,128)}) %all-reduce.19.cloned.1.call-update) | async-done | bytes 524304 | tf_op jit(solution)/shard_map/psum | solution.py:158
  1130.8 85.9 %all-reduce.21.cloned.1.call-done = f32[512,256]{1,0:T(8,128)} async-done(((f32[512,256]{1,0:T(8,128)}), f32[512,256]{1,0:T(8,128)}) %all-reduce.21.cloned.1.call-update) | async-done | bytes 524304 | tf_op jit(solution)/shard_map/psum | solution.py:158
  1224.6 6.3 scatter.16
  1230.9 132.8 %all-reduce.23.cloned.1.call-done = f32[256,256]{0,1:T(8,128)} async-done(((f32[256,256]{0,1:T(8,128)}), f32[256,256]{0,1:T(8,128)}) %all-reduce.23.cloned.1.call-update) | async-done | bytes 262160 | tf_op jit(solution)/shard_map/psum | solution.py:161
  1365.8 11.7 cholesky.446
  1377.6 9.8 custom-call.51
  1387.9 11.7 cholesky.456
  1408.3 11.7 cholesky.167
  1420.2 9.8 custom-call.37
  1432.5 11.9 cholesky.190
  1445.8 9.8 custom-call.38
  1457.1 11.7 cholesky.294
  1469.6 9.8 custom-call.52
  1480.9 11.9 cholesky.307
  1496.2 10.6 while.35
  1506.8 40.2 %custom-call.39 = f32[4,128,128]{1,2,0:T(8,128)S(1)} custom-call(f32[4,128,128]{2,1,0:T(8,128)} %get-tuple-element.288), custom_call_target="InvertDiagBlocksLowerTriangular" | custom-call | tf_op jit(solution)/shard_map/triangular_solve | solution.py:180
  1555.4 4.9 fusion.36
  (397 shorter events, 318.9 us)
Async XLA Ops:
  6.5 150.4 %all-reduce.11.cloned.1.call-start = ((), (), s32[]{:S(2)}) async-start(), calls=%async_computation | async-start | bytes 524288 | tf_op jit(solution)/shard_map/psum | solution.py:148
  10.2 519.9 %all-reduce.13.cloned.1.call-start = ((), (), s32[]{:S(2)}) async-start(), calls=%async_computation.1 | async-start | bytes 524288 | tf_op jit(solution)/shard_map/psum | solution.py:158
  238.0 15.6 collective-permute-start
  241.3 13.3 collective-permute-start.2
  246.6 6.2 collective-permute-start.3
  259.6 11.3 collective-permute-start.4
  260.9 14.9 collective-permute-start.5
  281.5 15.3 collective-permute-start.10
  289.8 9.0 collective-permute-start.11
  291.1 8.4 collective-permute-start.12
  294.2 6.9 collective-permute-start.13
  295.5 9.3 collective-permute-start.14
  296.8 12.0 collective-permute-start.15
  309.4 54.3 %collective-permute-start.16 = (bf16[7,256,256]{1,2,0:T(8,128)(2,1)}, bf16[7,256,256]{1,2,0:T(8,128)(2,1)}, u32[]{:S(2)}, u32[]{:S(2)}) collective-permute-start(bf16[7,256,256]{1,2,0:T(8,128)(2,1)} %bitcast_dynamic-update-slice_fusion.25), channel_id=1, source_target_pairs={{0,48},{16,64},{32,80},{48,96},{64,112},{1,49},{17,65},{33,81},{49... | collective-permute-start | bytes 2752520 | tf_op jit(solution)/shard_map/ppermute | solution.py:16
  316.5 50.7 %collective-permute-start.17 = (bf16[7,256,256]{1,2,0:T(8,128)(2,1)}, bf16[7,256,256]{1,2,0:T(8,128)(2,1)}, u32[]{:S(2)}, u32[]{:S(2)}) collective-permute-start(bf16[7,256,256]{1,2,0:T(8,128)(2,1)} %bitcast_dynamic-update-slice_fusion.25), channel_id=1, source_target_pairs={{0,32},{16,48},{32,64},{48,80},{64,96},{80,112},{1,33},{17,49},{33... | collective-permute-start | bytes 2752520 | tf_op jit(solution)/shard_map/ppermute | solution.py:16
  319.5 38.6 %collective-permute-start.6 = (bf16[1,1,768,256]{2,3,1,0:T(8,128)(2,1)}, bf16[1,1,768,256]{2,3,1,0:T(8,128)(2,1)}, u32[]{:S(2)}, u32[]{:S(2)}) collective-permute-start(bf16[1,1,768,256]{2,3,1,0:T(8,128)(2,1)} %convert_bitcast_fusion.1), channel_id=1, source_target_pairs={{0,16},{16,32},{32,48},{48,64},{64,80},{80,96},{96,112},{1,17},{17... | collective-permute-start | bytes 1179656 | tf_op jit(solution)/shard_map/ppermute | solution.py:24
  321.5 38.6 %collective-permute-start.7 = (bf16[1,1,768,256]{2,3,1,0:T(8,128)(2,1)}, bf16[1,1,768,256]{2,3,1,0:T(8,128)(2,1)}, u32[]{:S(2)}, u32[]{:S(2)}) collective-permute-start(bf16[1,1,768,256]{2,3,1,0:T(8,128)(2,1)} %convert_bitcast_fusion.1), channel_id=1, source_target_pairs={{16,0},{32,16},{48,32},{64,48},{80,64},{96,80},{112,96},{17,1},{33... | collective-permute-start | bytes 1179656 | tf_op jit(solution)/shard_map/ppermute | solution.py:27
  324.6 49.8 %collective-permute-start.18 = (bf16[7,256,256]{1,2,0:T(8,128)(2,1)}, bf16[7,256,256]{1,2,0:T(8,128)(2,1)}, u32[]{:S(2)}, u32[]{:S(2)}) collective-permute-start(bf16[7,256,256]{1,2,0:T(8,128)(2,1)} %bitcast_dynamic-update-slice_fusion.25), channel_id=1, source_target_pairs={{0,16},{16,32},{32,48},{48,64},{64,80},{80,96},{96,112},{1,17},{17... | collective-permute-start | bytes 2752520 | tf_op jit(solution)/shard_map/ppermute | solution.py:16
  358.1 23.7 %collective-permute-start.19 = (bf16[7,256,256]{1,2,0:T(8,128)(2,1)}, bf16[7,256,256]{1,2,0:T(8,128)(2,1)S(1)}, u32[]{:S(2)}, u32[]{:S(2)}) collective-permute-start(bf16[7,256,256]{1,2,0:T(8,128)(2,1)} %bitcast_dynamic-update-slice_fusion.25), channel_id=1, source_target_pairs={{16,0},{32,16},{48,32},{64,48},{80,64},{96,80},{112,96},{17,1},{33... | collective-permute-start | bytes 2752520 | tf_op jit(solution)/shard_map/ppermute | solution.py:16
  360.1 25.7 %collective-permute-start.20 = (bf16[7,256,256]{1,2,0:T(8,128)(2,1)}, bf16[7,256,256]{1,2,0:T(8,128)(2,1)S(1)}, u32[]{:S(2)}, u32[]{:S(2)}) collective-permute-start(bf16[7,256,256]{1,2,0:T(8,128)(2,1)} %bitcast_dynamic-update-slice_fusion.25), channel_id=1, source_target_pairs={{32,0},{48,16},{64,32},{80,48},{96,64},{112,80},{33,1},{49,17},{65... | collective-permute-start | bytes 2752520 | tf_op jit(solution)/shard_map/ppermute | solution.py:16
  363.7 23.0 %collective-permute-start.21 = (bf16[7,256,256]{1,2,0:T(8,128)(2,1)}, bf16[7,256,256]{1,2,0:T(8,128)(2,1)S(1)}, u32[]{:S(2)}, u32[]{:S(2)}) collective-permute-start(bf16[7,256,256]{1,2,0:T(8,128)(2,1)} %bitcast_dynamic-update-slice_fusion.25), channel_id=1, source_target_pairs={{48,0},{64,16},{80,32},{96,48},{112,64},{49,1},{65,17},{81,33},{97... | collective-permute-start | bytes 2752520 | tf_op jit(solution)/shard_map/ppermute | solution.py:16
  367.2 45.4 %collective-permute-start.8 = (bf16[3,1,768,256]{2,3,1,0:T(8,128)(2,1)}, bf16[3,1,768,256]{2,3,1,0:T(8,128)(2,1)}, u32[]{:S(2)}, u32[]{:S(2)}) collective-permute-start(bf16[3,1,768,256]{2,3,1,0:T(8,128)(2,1)} %pad_maximum_fusion.2), channel_id=1, source_target_pairs={{0,1},{1,2},{2,3},{3,4},{4,5},{5,6},{6,7},{7,8},{8,9},{9,10},{10,1... | collective-permute-start | bytes 3538952 | tf_op jit(solution)/shard_map/ppermute | solution.py:24
  374.4 38.2 %collective-permute-start.9 = (bf16[3,1,768,256]{2,3,1,0:T(8,128)(2,1)}, bf16[3,1,768,256]{2,3,1,0:T(8,128)(2,1)}, u32[]{:S(2)}, u32[]{:S(2)}) collective-permute-start(bf16[3,1,768,256]{2,3,1,0:T(8,128)(2,1)} %pad_maximum_fusion.2), channel_id=1, source_target_pairs={{1,0},{2,1},{3,2},{4,3},{5,4},{6,5},{7,6},{8,7},{9,8},{10,9},{11,1... | collective-permute-start | bytes 3538952 | tf_op jit(solution)/shard_map/ppermute | solution.py:27
  428.5 189.4 %all-reduce.15.cloned.1.call-start = ((), (), s32[]{:S(2)}) async-start(), calls=%async_computation.2 | async-start | bytes 524288 | tf_op jit(solution)/shard_map/psum | solution.py:158
  530.1 234.8 %all-reduce.17.cloned.1.call-start = ((), (), s32[]{:S(2)}) async-start(), calls=%async_computation.3 | async-start | bytes 524288 | tf_op jit(solution)/shard_map/psum | solution.py:161
  622.6 505.5 %all-reduce.19.cloned.1.call-start = ((), (), s32[]{:S(2)}) async-start(), calls=%async_computation.4 | async-start | bytes 1048576 | tf_op jit(solution)/shard_map/psum | solution.py:158
  853.8 9.9 collective-permute-start.22
  856.4 11.2 collective-permute-start.23
  868.8 8.4 collective-permute-start.24
  870.2 9.3 collective-permute-start.25
  882.3 16.7 %collective-permute-start.30 = (bf16[256,256]{0,1:T(8,128)(2,1)S(1)}, bf16[256,256]{0,1:T(8,128)(2,1)S(1)}, u32[]{:S(2)}, u32[]{:S(2)}) collective-permute-start(bf16[256,256]{0,1:T(8,128)(2,1)S(1)} %bitcast.418), channel_id=1, source_target_pairs={{0,3},{1,4},{2,5},{3,6},{4,7},{5,8},{6,9},{7,10},{8,11},{9,12},{10... | collective-permute-start | bytes 393224 | tf_op jit(solution)/shard_map/ppermute | solution.py:16
  891.9 9.0 collective-permute-start.31
  893.5 8.1 collective-permute-start.32
  896.3 6.7 collective-permute-start.33
  897.6 10.8 collective-permute-start.34
  899.0 12.3 collective-permute-start.35
  911.9 52.9 %collective-permute-start.36 = (bf16[7,256,256]{1,2,0:T(8,128)(2,1)}, bf16[7,256,256]{1,2,0:T(8,128)(2,1)}, u32[]{:S(2)}, u32[]{:S(2)}) collective-permute-start(bf16[7,256,256]{1,2,0:T(8,128)(2,1)} %bitcast_dynamic-update-slice_fusion.19), channel_id=1, source_target_pairs={{0,48},{16,64},{32,80},{48,96},{64,112},{1,49},{17,65},{33,81},{49... | collective-permute-start | bytes 2752520 | tf_op jit(solution)/shard_map/ppermute | solution.py:16
  920.2 48.1 %collective-permute-start.37 = (bf16[7,256,256]{1,2,0:T(8,128)(2,1)}, bf16[7,256,256]{1,2,0:T(8,128)(2,1)}, u32[]{:S(2)}, u32[]{:S(2)}) collective-permute-start(bf16[7,256,256]{1,2,0:T(8,128)(2,1)} %bitcast_dynamic-update-slice_fusion.19), channel_id=1, source_target_pairs={{0,32},{16,48},{32,64},{48,80},{64,96},{80,112},{1,33},{17,49},{33... | collective-permute-start | bytes 2752520 | tf_op jit(solution)/shard_map/ppermute | solution.py:16
  922.5 38.0 %collective-permute-start.26 = (bf16[1,1,768,256]{2,3,1,0:T(8,128)(2,1)S(1)}, bf16[1,1,768,256]{2,3,1,0:T(8,128)(2,1)S(1)}, u32[]{:S(2)}, u32[]{:S(2)}) collective-permute-start(bf16[1,1,768,256]{2,3,1,0:T(8,128)(2,1)S(1)} %convert_bitcast_fusion), channel_id=1, source_target_pairs={{0,16},{16,32},{32,48},{48,64},{64,80},{80,96},{96,112},{1,17},{17... | collective-permute-start | bytes 1179656 | tf_op jit(solution)/shard_map/ppermute | solution.py:24
  924.4 38.0 %collective-permute-start.27 = (bf16[1,1,768,256]{2,3,1,0:T(8,128)(2,1)S(1)}, bf16[1,1,768,256]{2,3,1,0:T(8,128)(2,1)S(1)}, u32[]{:S(2)}, u32[]{:S(2)}) collective-permute-start(bf16[1,1,768,256]{2,3,1,0:T(8,128)(2,1)S(1)} %convert_bitcast_fusion), channel_id=1, source_target_pairs={{16,0},{32,16},{48,32},{64,48},{80,64},{96,80},{112,96},{17,1},{33... | collective-permute-start | bytes 1179656 | tf_op jit(solution)/shard_map/ppermute | solution.py:27
  926.8 48.7 %collective-permute-start.38 = (bf16[7,256,256]{1,2,0:T(8,128)(2,1)}, bf16[7,256,256]{1,2,0:T(8,128)(2,1)}, u32[]{:S(2)}, u32[]{:S(2)}) collective-permute-start(bf16[7,256,256]{1,2,0:T(8,128)(2,1)} %bitcast_dynamic-update-slice_fusion.19), channel_id=1, source_target_pairs={{0,16},{16,32},{32,48},{48,64},{64,80},{80,96},{96,112},{1,17},{17... | collective-permute-start | bytes 2752520 | tf_op jit(solution)/shard_map/ppermute | solution.py:16
  960.5 23.7 %collective-permute-start.39 = (bf16[7,256,256]{1,2,0:T(8,128)(2,1)}, bf16[7,256,256]{1,2,0:T(8,128)(2,1)S(1)}, u32[]{:S(2)}, u32[]{:S(2)}) collective-permute-start(bf16[7,256,256]{1,2,0:T(8,128)(2,1)} %bitcast_dynamic-update-slice_fusion.19), channel_id=1, source_target_pairs={{16,0},{32,16},{48,32},{64,48},{80,64},{96,80},{112,96},{17,1},{33... | collective-permute-start | bytes 2752520 | tf_op jit(solution)/shard_map/ppermute | solution.py:16
  962.4 25.7 %collective-permute-start.40 = (bf16[7,256,256]{1,2,0:T(8,128)(2,1)}, bf16[7,256,256]{1,2,0:T(8,128)(2,1)S(1)}, u32[]{:S(2)}, u32[]{:S(2)}) collective-permute-start(bf16[7,256,256]{1,2,0:T(8,128)(2,1)} %bitcast_dynamic-update-slice_fusion.19), channel_id=1, source_target_pairs={{32,0},{48,16},{64,32},{80,48},{96,64},{112,80},{33,1},{49,17},{65... | collective-permute-start | bytes 2752520 | tf_op jit(solution)/shard_map/ppermute | solution.py:16
  964.8 24.2 %collective-permute-start.41 = (bf16[7,256,256]{1,2,0:T(8,128)(2,1)}, bf16[7,256,256]{1,2,0:T(8,128)(2,1)S(1)}, u32[]{:S(2)}, u32[]{:S(2)}) collective-permute-start(bf16[7,256,256]{1,2,0:T(8,128)(2,1)} %bitcast_dynamic-update-slice_fusion.19), channel_id=1, source_target_pairs={{48,0},{64,16},{80,32},{96,48},{112,64},{49,1},{65,17},{81,33},{97... | collective-permute-start | bytes 2752520 | tf_op jit(solution)/shard_map/ppermute | solution.py:16
  968.3 44.0 %collective-permute-start.28 = (bf16[3,1,768,256]{2,3,1,0:T(8,128)(2,1)}, bf16[3,1,768,256]{2,3,1,0:T(8,128)(2,1)}, u32[]{:S(2)}, u32[]{:S(2)}) collective-permute-start(bf16[3,1,768,256]{2,3,1,0:T(8,128)(2,1)} %pad_maximum_fusion.3), channel_id=1, source_target_pairs={{0,1},{1,2},{2,3},{3,4},{4,5},{5,6},{6,7},{7,8},{8,9},{9,10},{10,1... | collective-permute-start | bytes 3538952 | tf_op jit(solution)/shard_map/ppermute | solution.py:24
  975.6 36.7 %collective-permute-start.29 = (bf16[3,1,768,256]{2,3,1,0:T(8,128)(2,1)}, bf16[3,1,768,256]{2,3,1,0:T(8,128)(2,1)}, u32[]{:S(2)}, u32[]{:S(2)}) collective-permute-start(bf16[3,1,768,256]{2,3,1,0:T(8,128)(2,1)} %pad_maximum_fusion.3), channel_id=1, source_target_pairs={{1,0},{2,1},{3,2},{4,3},{5,4},{6,5},{7,6},{8,7},{9,8},{10,9},{11,1... | collective-permute-start | bytes 3538952 | tf_op jit(solution)/shard_map/ppermute | solution.py:27
  1027.6 189.1 %all-reduce.21.cloned.1.call-start = ((), (), s32[]{:S(2)}) async-start(), calls=%async_computation.5 | async-start | bytes 1048576 | tf_op jit(solution)/shard_map/psum | solution.py:158
  1128.1 235.6 %all-reduce.23.cloned.1.call-start = ((), (), s32[]{:S(2)}) async-start(), calls=%async_computation.6 | async-start | bytes 524288 | tf_op jit(solution)/shard_map/psum | solution.py:161
  (46 other events, 1467.9 us)
Sparse Core Ops, SparseCore 0:
  12.1 144.7 all-reduce.10
  428.6 101.4 all-reduce.12
  533.6 84.2 all-reduce.14
  622.8 142.1 all-reduce.16
  1027.7 100.3 all-reduce.18
  1131.5 85.1 all-reduce.20
  1221.5 142.1 all-reduce.22
